TPU v7x, 32 devices: a whole 2x2x4 slice. The times are simulated.
32 devices in a mesh: row: 4 (over y, x), col: 8 (over z, core).
Axes of the slice: x: 2, y: 2, z: 4, core: 2. Of those that a mesh axis runs over, the one named last changes fastest.
Arguments:
- frames: bfloat16 [256, 8192], P('col', 'row'), may hold values from -6 to 6
- cotangent: bfloat16 [256, 8192], P('col', 'row'), may hold values from -6 to 6
- gate_weight: bfloat16 [8192, 14336], P('row', 'col'), may hold values from -0.0625 to 0.0625
- up_weight: bfloat16 [8192, 14336], P('row', 'col'), may hold values from -0.0625 to 0.0625
- down_weight: bfloat16 [14336, 8192], P('col', 'row'), may hold values from -0.046875 to 0.046875
- utt_ids: int32 [256], replicated, may hold values from 0 to 15, never falling along the last dimension, each value on 1 to 32 neighbouring positions
- valid_len: int32 [16], replicated, may hold values from 1 to 32
- time_start: int32 [16], replicated, may hold values from 0 to 31
- time_width: int32 [16], replicated, may hold values from 0 to 8
- freq_start: int32 [16], replicated, may hold values from 0 to 8191
- freq_width: int32 [16], replicated, may hold values from 0 to 2048
Outputs:
- output: bfloat16 [256, 8192], P('col', 'row')
- grad_frames: bfloat16 [256, 8192], P('col', 'row')
- grad_gate: bfloat16 [8192, 14336], P('row', 'col')
- grad_up: bfloat16 [8192, 14336], P('row', 'col')
- grad_down: bfloat16 [14336, 8192], P('col', 'row')
Inputs may be any that keep to these rules, and one draw needn't show every extreme that they name: `utt_ids`: token ids never fall along the tokens; each utterance holds 1 to 32 tokens.
All inputs are finite; a program needn't handle non-finite values.
Results may differ from a plain program's by a relative error of at most 0.025.
Values may be sent and summed in bfloat16 or wider, within the bound.
A program may use at most 128 MiB of HBM per device.

v0:
```python
import jax
import jax.numpy as jnp
from jax import lax
from jax.sharding import PartitionSpec as P


def span_masks(
    utt_ids,
    local_ids,
    tok_index,
    feat_index,
    valid_len,
    time_start,
    time_width,
    freq_start,
    freq_width,
):
    utt_index = jnp.arange(valid_len.shape[0], dtype=jnp.int32)
    starts = jnp.sum((utt_ids[None, :] < utt_index[:, None]).astype(jnp.int32), axis=1)
    member = (local_ids[:, None] == utt_index[None, :]).astype(jnp.int32)

    def lookup(table):
        return jnp.sum(member * table[None, :], axis=1)

    position = tok_index - lookup(starts)
    valid_rows = position < lookup(valid_len)
    time_low = lookup(time_start)
    in_time = (position >= time_low) & (position < time_low + lookup(time_width))
    freq_low = lookup(freq_start)[:, None]
    freq_high = freq_low + lookup(freq_width)[:, None]
    in_freq = (feat_index[None, :] >= freq_low) & (feat_index[None, :] < freq_high)
    keep_mask = (valid_rows & jnp.logical_not(in_time))[:, None] & jnp.logical_not(in_freq)
    return (keep_mask, valid_rows)


def shards(
    frames,
    cotangent,
    gate_weight,
    up_weight,
    down_weight,
    utt_ids,
    valid_len,
    time_start,
    time_width,
    freq_start,
    freq_width,
):
    tok_rows, feat_cols = frames.shape
    hidden_cols = gate_weight.shape[1]
    first_tok = lax.axis_index("col") * tok_rows
    first_feat = lax.axis_index("row") * feat_cols
    tok_index = first_tok + jnp.arange(tok_rows, dtype=jnp.int32)
    feat_index = first_feat + jnp.arange(feat_cols, dtype=jnp.int32)
    local_ids = lax.dynamic_slice_in_dim(utt_ids, first_tok, tok_rows)
    keep_mask, valid_rows = span_masks(
        utt_ids,
        local_ids,
        tok_index,
        feat_index,
        valid_len,
        time_start,
        time_width,
        freq_start,
        freq_width,
    )
    masked = jnp.where(keep_mask, frames, jnp.zeros_like(frames))
    cot_valid = jnp.where(valid_rows[:, None], cotangent, jnp.zeros_like(cotangent))
    contract_last = (((1,), (1,)), ((), ()))
    contract_first = (((0,), (0,)), ((), ()))
    tokens_all = lax.all_gather(masked, "col", axis=0, tiled=True)
    block = tokens_all
    gate_up = lax.psum_scatter(
        jnp.concatenate(
            [
                jnp.dot(block, gate_weight, preferred_element_type=jnp.float32),
                jnp.dot(block, up_weight, preferred_element_type=jnp.float32),
            ],
            axis=1,
        ).astype(jnp.bfloat16),
        "row",
        scatter_dimension=0,
        tiled=True,
    ).astype(jnp.float32)
    gate = gate_up[:, :hidden_cols]
    up = gate_up[:, hidden_cols:]
    sigmoid_gate = jax.nn.sigmoid(gate)
    hidden = (gate * sigmoid_gate * up).astype(jnp.bfloat16)
    hidden_all = lax.all_gather(hidden, "row", axis=0, tiled=True)
    block = hidden_all
    output = lax.psum_scatter(
        jnp.dot(block, down_weight, preferred_element_type=jnp.float32).astype(jnp.bfloat16),
        "col",
        scatter_dimension=0,
        tiled=True,
    )
    cot_all = lax.all_gather(cot_valid, "col", axis=0, tiled=True)
    block = cot_all
    grad_hidden = lax.psum_scatter(
        lax.dot_general(
            block, down_weight, contract_last, preferred_element_type=jnp.float32
        ).astype(jnp.bfloat16),
        "row",
        scatter_dimension=0,
        tiled=True,
    ).astype(jnp.float32)
    dgate = (grad_hidden * up * sigmoid_gate * (1.0 + gate * (1.0 - sigmoid_gate))).astype(
        jnp.bfloat16
    )
    dup = (grad_hidden * gate * sigmoid_gate).astype(jnp.bfloat16)
    dgate_all, dup_all = (
        lax.all_gather(dgate, "row", axis=0, tiled=True),
        lax.all_gather(dup, "row", axis=0, tiled=True),
    )
    grad_down = lax.dot_general(
        hidden_all, cot_all, contract_first, preferred_element_type=jnp.float32
    ).astype(jnp.bfloat16)
    grad_gate = lax.dot_general(
        tokens_all, dgate_all, contract_first, preferred_element_type=jnp.float32
    ).astype(jnp.bfloat16)
    grad_up = lax.dot_general(
        tokens_all, dup_all, contract_first, preferred_element_type=jnp.float32
    ).astype(jnp.bfloat16)
    grad_masked = lax.psum_scatter(
        (
            lax.dot_general(
                dgate_all, gate_weight, contract_last, preferred_element_type=jnp.float32
            )
            + lax.dot_general(dup_all, up_weight, contract_last, preferred_element_type=jnp.float32)
        ).astype(jnp.bfloat16),
        "col",
        scatter_dimension=0,
        tiled=True,
    ).astype(jnp.float32)
    grad_frames = jnp.where(keep_mask, grad_masked, jnp.zeros_like(grad_masked)).astype(
        jnp.bfloat16
    )
    return (output, grad_frames, grad_gate, grad_up, grad_down)


def solution(mesh):
    placed = (
        P("col", "row"),
        P("col", "row"),
        P("row", "col"),
        P("row", "col"),
        P("col", "row"),
        P(),
        P(),
        P(),
        P(),
        P(),
        P(),
    )
    return jax.shard_map(
        shards,
        mesh=mesh,
        in_specs=placed,
        out_specs=(
            P("col", "row"),
            P("col", "row"),
            P("row", "col"),
            P("row", "col"),
            P("col", "row"),
        ),
        check_vma=False,
    )
```

profile of v0, /device:TPU:0, one launch (start us, length us, event | category | flops | bytes accessed | tf_op | source)
XLA Modules:
  0.0 233.6 jit_solution(2361530849330241817)
XLA Ops:
  7.2 0.0 all-gather.3.cloned.1.call-start
  7.2 0.8 convert_reduce_fusion
  8.0 0.8 dynamic_slice.3
  8.8 0.8 select_reduce_fusion.4
  9.6 1.7 broadcast_select_fusion.1
  11.3 0.0 all-gather.3.cloned.1.call-update
  11.4 0.0 all-gather.5.cloned.1.call-start
  11.4 1.6 broadcast_select_fusion
  13.1 0.0 all-gather.5.cloned.1.call-update
  13.1 0.0 reduce-scatter.5.cloned.1.call-start
  13.1 23.2 %all-gather.3.cloned.1.call-done = bf16[256,2048]{1,0:T(8,128)(2,1)} async-done(((bf16[32,2048]{1,0:T(8,128)(2,1)}), bf16[256,2048]{1,0:T(8,128)(2,1)}) %all-gather.3.cloned.1.call-update) | async-done | bytes 1048592 | tf_op jit(solution)/shard_map/all_gather | solution.py:71
  36.3 0.0 copy-start
  36.3 5.5 %convolution_convert_fusion.5 = bf16[256,1792]{1,0:T(8,128)(2,1)S(1)} fusion(bf16[256,2048]{1,0:T(8,128)(2,1)} %all-gather.3.cloned.1.call-done, bf16[2048,1792]{1,0:T(8,128)(2,1)} %param.14), kind=kOutput, calls=%fused_computation.6 | convolution fusion | flops 1879506944 | bytes 9306112 | tf_op jit(solution)/shard_map/dot_general | solution.py:77
  41.9 0.0 copy-done
  41.9 5.2 %convolution_convert_fusion.6 = bf16[256,1792]{1,0:T(8,128)(2,1)S(1)} fusion(bf16[256,2048]{1,0:T(8,128)(2,1)S(1)} %copy-done, bf16[2048,1792]{1,0:T(8,128)(2,1)} %param.13), kind=kOutput, calls=%fused_computation.7 | convolution fusion | flops 1879506944 | bytes 9306112 | tf_op jit(solution)/shard_map/dot_general | solution.py:76
  47.0 1.4 pad_maximum_fusion
  48.4 0.0 reduce-scatter.5.cloned.1.call-update
  48.4 0.0 reduce-scatter.9.cloned.1.call-start
  48.5 11.8 %all-gather.5.cloned.1.call-done = bf16[256,2048]{1,0:T(8,128)(2,1)} async-done(((bf16[32,2048]{1,0:T(8,128)(2,1)}), bf16[256,2048]{1,0:T(8,128)(2,1)}) %all-gather.5.cloned.1.call-update) | async-done | bytes 1048592 | tf_op jit(solution)/shard_map/all_gather | solution.py:97
  60.2 6.4 %convolution_convert_fusion.3 = bf16[256,1792]{1,0:T(8,128)(2,1)} fusion(bf16[256,2048]{1,0:T(8,128)(2,1)} %all-gather.5.cloned.1.call-done, bf16[1792,2048]{1,0:T(8,128)(2,1)} %param.15), kind=kOutput, calls=%fused_computation.4 | convolution fusion | flops 1879506944 | bytes 9306112 | tf_op jit(solution)/shard_map/dot_general | solution.py:100
  66.7 0.0 reduce-scatter.9.cloned.1.call-update
  66.7 0.0 reduce-scatter.11.cloned.1.call-start
  66.8 29.8 %reduce-scatter.5.cloned.1.call-done = bf16[64,3584]{1,0:T(8,128)(2,1)} async-done(((bf16[256,3584]{1,0:T(8,128)(2,1)}), bf16[64,3584]{1,0:T(8,128)(2,1)}) %reduce-scatter.5.cloned.1.call-update) | async-done | bytes 458768 | tf_op jit(solution)/shard_map/reduce_scatter | solution.py:73
  96.5 1.1 convert_element_type.45
  97.6 29.2 %reduce-scatter.9.cloned.1.call-done = bf16[64,1792]{1,0:T(8,128)(2,1)} async-done(((bf16[256,1792]{1,0:T(8,128)(2,1)}), bf16[64,1792]{1,0:T(8,128)(2,1)}) %reduce-scatter.9.cloned.1.call-update) | async-done | bytes 229392 | tf_op jit(solution)/shard_map/reduce_scatter | solution.py:99
  126.8 1.2 fusion.5
  128.0 0.0 slice-start
  128.0 12.6 %all_gather.19 = bf16[256,1792]{1,0:T(8,128)(2,1)S(1)} all-gather(bf16[64,1792]{1,0:T(8,128)(2,1)S(1)} %get-tuple-element.11), channel_id=1, replica_groups=mesh['row'=4,'col'=8] {'row'}, dimensions={0}, use_global_device_ids=true | all-gather | bytes 1146880 | tf_op jit(solution)/shard_map/all_gather | solution.py:113
  140.6 0.0 copy-start.1
  140.6 11.4 %all_gather.18 = bf16[256,1792]{1,0:T(8,128)(2,1)S(1)} all-gather(bf16[64,1792]{1,0:T(8,128)(2,1)S(1)} %get-tuple-element.12), channel_id=1, replica_groups=mesh['row'=4,'col'=8] {'row'}, dimensions={0}, use_global_device_ids=true | all-gather | bytes 1146880 | tf_op jit(solution)/shard_map/all_gather | solution.py:112
  152.0 0.0 slice-start.1
  152.0 5.3 %fusion.7 = f32[256,2048]{1,0:T(8,128)S(1)} fusion(bf16[256,1792]{1,0:T(8,128)(2,1)S(1)} %all_gather.18, bf16[2048,1792]{1,0:T(8,128)(2,1)} %param.13), kind=kOutput, calls=%fused_computation.36 | convolution fusion | flops 1879048192 | bytes 10354688 | tf_op jit(solution)/shard_map/dot_general | solution.py:126
  157.3 0.0 slice-done
  157.3 0.0 slice-done.1
  157.3 3.1 %fusion = bf16[256,2048]{1,0:T(8,128)(2,1)} fusion(f32[256,2048]{1,0:T(8,128)S(1)} %fusion.7, bf16[256,1792]{1,0:T(8,128)(2,1)S(1)} %all_gather.19, bf16[2048,1792]{1,0:T(8,128)(2,1)S(1)} %bitcast.19), kind=kOutput, calls=%fused_computation.8 | convolution fusion | flops 1880096768 | bytes 11403264 | tf_op jit(solution)/shard_map/dot_general | solution.py:129
  160.4 0.0 copy-done.1
  160.4 0.0 reduce-scatter.11.cloned.1.call-update
  160.5 0.0 reduce-scatter.7.cloned.1.call-start
  160.5 12.6 %all_gather.16 = bf16[256,1792]{1,0:T(8,128)(2,1)S(1)} all-gather(bf16[64,1792]{1,0:T(8,128)(2,1)S(1)} %get-tuple-element.13), channel_id=1, replica_groups=mesh['row'=4,'col'=8] {'row'}, dimensions={0}, use_global_device_ids=true | all-gather | bytes 1146880 | tf_op jit(solution)/shard_map/all_gather | solution.py:89
  173.1 6.2 %convolution_convert_fusion.4 = bf16[256,2048]{1,0:T(8,128)(2,1)} fusion(bf16[256,1792]{1,0:T(8,128)(2,1)S(1)} %all_gather.16, bf16[1792,2048]{1,0:T(8,128)(2,1)} %param.15), kind=kOutput, calls=%fused_computation.5 | convolution fusion | flops 1879572480 | bytes 9306112 | tf_op jit(solution)/shard_map/dot_general | solution.py:92
  179.3 0.0 reduce-scatter.7.cloned.1.call-update
  179.4 0.0 copy-start.2
  179.4 6.5 %convolution_convert_fusion = bf16[1792,2048]{1,0:T(8,128)(2,1)} fusion(bf16[256,1792]{1,0:T(8,128)(2,1)S(1)} %all_gather.16, bf16[256,2048]{1,0:T(8,128)(2,1)} %all-gather.5.cloned.1.call-done), kind=kOutput, calls=%fused_computation | convolution fusion | flops 1882718208 | bytes 9306112 | tf_op jit(solution)/shard_map/dot_general | solution.py:115
  185.8 0.0 copy-done.2
  185.8 5.2 %convolution_convert_fusion.1 = bf16[2048,1792]{1,0:T(8,128)(2,1)} fusion(bf16[256,2048]{1,0:T(8,128)(2,1)S(1)} %copy-done, bf16[256,1792]{1,0:T(8,128)(2,1)S(1)} %copy-done.2), kind=kOutput, calls=%fused_computation.1 | convolution fusion | flops 1882718208 | bytes 9306112 | tf_op jit(solution)/shard_map/dot_general | solution.py:121
  191.0 5.2 %convolution_convert_fusion.2 = bf16[2048,1792]{1,0:T(8,128)(2,1)} fusion(bf16[256,2048]{1,0:T(8,128)(2,1)S(1)} %copy-done, bf16[256,1792]{1,0:T(8,128)(2,1)S(1)} %all_gather.18), kind=kOutput, calls=%fused_computation.2 | convolution fusion | flops 1882718208 | bytes 9306112 | tf_op jit(solution)/shard_map/dot_general | solution.py:118
  196.2 1.7 select_convert_fusion
  197.9 28.8 %reduce-scatter.7.cloned.1.call-done = bf16[32,2048]{1,0:T(8,128)(2,1)} async-done(((bf16[256,2048]{1,0:T(8,128)(2,1)}), bf16[32,2048]{1,0:T(8,128)(2,1)}) %reduce-scatter.7.cloned.1.call-update) | async-done | bytes 131088 | tf_op jit(solution)/shard_map/reduce_scatter | solution.py:91
  (5 shorter events, 0.0 us)
Async XLA Ops:
  7.2 29.1 %all-gather.3.cloned.1.call-start = ((), (), s32[]{:S(2)}) async-start(), calls=%async_computation.4 | async-start | bytes 1179648 | tf_op jit(solution)/shard_map/all_gather | solution.py:71
  11.4 48.9 %all-gather.5.cloned.1.call-start = ((), (), s32[]{:S(2)}) async-start(), calls=%async_computation.7 | async-start | bytes 1179648 | tf_op jit(solution)/shard_map/all_gather | solution.py:97
  13.1 83.5 %reduce-scatter.5.cloned.1.call-start = ((), (), s32[]{:S(2)}) async-start(), calls=%async_computation.5 | async-start | bytes 2293760 | tf_op jit(solution)/shard_map/reduce_scatter | solution.py:73
  36.3 5.6 %copy-start = (bf16[256,2048]{1,0:T(8,128)(2,1)S(1)}, bf16[256,2048]{1,0:T(8,128)(2,1)}, u32[]{:S(2)}) copy-start(bf16[256,2048]{1,0:T(8,128)(2,1)} %all-gather.3.cloned.1.call-done) | copy-start | bytes 3145732
  48.4 78.4 %reduce-scatter.9.cloned.1.call-start = ((), (), s32[]{:S(2)}) async-start(), calls=%async_computation.8 | async-start | bytes 1146880 | tf_op jit(solution)/shard_map/reduce_scatter | solution.py:99
  66.7 129.5 %reduce-scatter.11.cloned.1.call-start = ((), (), s32[]{:S(2)}) async-start(), calls=%async_computation.9 | async-start | bytes 1179648 | tf_op jit(solution)/shard_map/reduce_scatter | solution.py:124
  128.0 29.3 %slice-start = ((s8[7340032]{0:T(1024)(128)(4,1)}), s8[4194304]{0:T(1024)(128)(4,1)S(1)}, s32[]{:S(2)}) async-start(s8[7340032]{0:T(1024)(128)(4,1)} %bitcast.18), calls=%async_computation.10 | async-start | bytes 8388608
  140.6 19.8 %copy-start.1 = (bf16[256,1792]{1,0:T(8,128)(2,1)}, bf16[256,1792]{1,0:T(8,128)(2,1)S(1)}, u32[]{:S(2)}) copy-start(bf16[256,1792]{1,0:T(8,128)(2,1)S(1)} %all_gather.19) | copy-start | bytes 2752516
  152.0 5.3 %slice-start.1 = ((s8[7340032]{0:T(1024)(128)(4,1)}), s8[3145728]{0:T(1024)(128)(4,1)S(1)}, s32[]{:S(2)}) async-start(s8[7340032]{0:T(1024)(128)(4,1)} %bitcast.18), calls=%async_computation.11 | async-start | bytes 6291456
  160.5 66.3 %reduce-scatter.7.cloned.1.call-start = ((), (), s32[]{:S(2)}) async-start(), calls=%async_computation.6 | async-start | bytes 1179648 | tf_op jit(solution)/shard_map/reduce_scatter | solution.py:91
  179.4 6.5 %copy-start.2 = (bf16[256,1792]{1,0:T(8,128)(2,1)S(1)}, bf16[256,1792]{1,0:T(8,128)(2,1)}, u32[]{:S(2)}) copy-start(bf16[256,1792]{1,0:T(8,128)(2,1)} %copy-done.1) | copy-start | bytes 2752516
Sparse Core Ops, SparseCore 0:
  11.5 24.7 all-gather.2
  38.5 21.7 all-gather.4
  63.9 32.6 reduce-scatter.4
  99.9 26.8 reduce-scatter.8
  160.6 32.7 reduce-scatter.10
  196.1 30.6 reduce-scatter.6
where the time goes:
time: 234 us
  waiting for transfers between devices  123 us (53%)
  matrix products  48.7 us (21%)
  blocking collectives  36.5 us (16%)
  between operations  14.2 us (6%)
  other arithmetic  10.3 us (4%)
    reduce_scatter x1, waiting for transfers between devices, shards(): lax.psum_scatter(jnp.concatenate([jnp.dot(block, gate_weight, preferred_e...  29.8 us
    reduce_scatter x1, waiting for transfers between devices, shards(): lax.psum_scatter(lax.dot_general(block, down_weight, contract_last, prefe...  29.2 us
    reduce_scatter x1, waiting for transfers between devices, shards(): lax.psum_scatter(jnp.dot(block, down_weight, preferred_element_type=jnp.f...  28.8 us
    all_gather x1, waiting for transfers between devices, shards(): tokens_all = lax.all_gather(masked, 'col', axis=0, tiled=True)  23.2 us
    all_gather x1, blocking collectives, shards(): lax.all_gather(dup, 'row', axis=0, tiled=True)  12.6 us
    all_gather x1, blocking collectives, shards(): hidden_all = lax.all_gather(hidden, 'row', axis=0, tiled=True)  12.6 us
    all_gather x1, waiting for transfers between devices, shards(): cot_all = lax.all_gather(cot_valid, 'col', axis=0, tiled=True)  11.8 us
    all_gather x1, blocking collectives, shards(): lax.all_gather(dgate, 'row', axis=0, tiled=True)  11.4 us
  transfers between devices with their start and end apart: 6, of which 5 were waited for; matrix products, arithmetic and copies ran while one was open for 20% of the time, Pallas kernels for 0%

commit v1 on v0

v1 whole, which is shorter than its diff:
```python
import functools
import jax
import jax.numpy as jnp
from jax import lax
from jax.experimental import pallas as pl
from jax.experimental.pallas import tpu as pltpu
from jax.sharding import PartitionSpec as P


def span_masks(
    utt_ids,
    local_ids,
    tok_index,
    feat_index,
    valid_len,
    time_start,
    time_width,
    freq_start,
    freq_width,
):
    utt_index = jnp.arange(valid_len.shape[0], dtype=jnp.int32)
    starts = jnp.sum((utt_ids[None, :] < utt_index[:, None]).astype(jnp.int32), axis=1)
    member = (local_ids[:, None] == utt_index[None, :]).astype(jnp.int32)

    def lookup(table):
        return jnp.sum(member * table[None, :], axis=1)

    position = tok_index - lookup(starts)
    valid_rows = position < lookup(valid_len)
    time_low = lookup(time_start)
    in_time = (position >= time_low) & (position < time_low + lookup(time_width))
    freq_low = lookup(freq_start)[:, None]
    freq_high = freq_low + lookup(freq_width)[:, None]
    in_freq = (feat_index[None, :] >= freq_low) & (feat_index[None, :] < freq_high)
    keep_mask = (valid_rows & jnp.logical_not(in_time))[:, None] & jnp.logical_not(in_freq)
    return (keep_mask, valid_rows)


MESH_ID = pl.DeviceIdType.MESH
LAST = (((1,), (1,)), ((), ()))
FIRST = (((0,), (0,)), ((), ()))
F32 = jnp.float32
BF16 = jnp.bfloat16


def dot(a, b):
    return jnp.dot(a, b, preferred_element_type=F32)


def dot_last(a, b):
    return lax.dot_general(a, b, LAST, preferred_element_type=F32)


def exchange_kernel(
    R,
    C,
    masked,
    cot,
    gate_hbm,
    up_hbm,
    down_hbm,
    out,
    gmask,
    tok_hbm,
    cotall_hbm,
    hid_hbm,
    dg_hbm,
    du_hbm,
    gw,
    uw,
    dw,
    rows,
    gu_send,
    gu_recv,
    gh_send,
    gh_recv,
    gate_s,
    up_s,
    act,
    part,
    sib_recv,
    z_send,
    z_recv,
    w_sem,
    o_sem,
    ag_s,
    ag_r,
    fw_s,
    fw_r,
    gu_ss,
    gu_rs,
    gh_ss,
    gh_rs,
    act_ss,
    act_rs,
    sib_ss,
    sib_rs,
    z_ss,
    z_rs,
):
    r = lax.axis_index("row")
    c = lax.axis_index("col")
    z = c // 2
    k = c % 2
    Z = C // 2
    sib = z * 2 + 1 - k
    nh, chunk = dw.shape[0], dw.shape[1]
    t = masked.shape[0]
    total = rows.shape[1]
    tq = total // R
    nd, dchunk = part.shape[1], part.shape[5]

    weights = []
    for i in range(nh):
        span = pl.ds(i * chunk, chunk)
        weights.append(
            [
                pltpu.make_async_copy(gate_hbm.at[:, span], gw.at[i], w_sem.at[0, i]),
                pltpu.make_async_copy(up_hbm.at[:, span], uw.at[i], w_sem.at[1, i]),
                pltpu.make_async_copy(down_hbm.at[span, :], dw.at[i], w_sem.at[2, i]),
            ]
        )

    barrier = pltpu.get_barrier_semaphore()
    for j in range(1, R):
        pl.semaphore_signal(
            barrier, inc=1, device_id=(lax.rem(r + j, R), c), device_id_type=MESH_ID
        )
    for j in range(1, Z):
        pl.semaphore_signal(
            barrier, inc=1, device_id=(r, lax.rem(z + j, Z) * 2 + k), device_id_type=MESH_ID
        )
    pl.semaphore_signal(barrier, inc=1, device_id=(r, sib), device_id_type=MESH_ID)
    pl.semaphore_wait(barrier, R + Z - 1)

    def block(x, index):
        return rows.at[x, pl.ds(pl.multiple_of(index * t, t), t), :]

    def remote(src, dst, ss, rs, dev):
        return pltpu.make_async_remote_copy(
            src_ref=src,
            dst_ref=dst,
            send_sem=ss,
            recv_sem=rs,
            device_id=dev,
            device_id_type=MESH_ID,
        )

    def gather_far(x, j):
        own = (masked, cot)[x]
        return remote(
            own,
            block(x, c),
            ag_s.at[x, j],
            ag_r.at[x, j],
            (r, lax.rem(z + j, Z) * 2 + k),
        )

    def gather_near(x, j):
        index = lax.rem(z - j + Z, Z) * 2 + k
        src = (masked, cot)[x] if j == 0 else block(x, index)
        return remote(src, block(x, index), fw_s.at[x, j], fw_r.at[x, j], (r, sib))

    for x in range(2):
        for j in range(1, Z):
            gather_far(x, j).start()
        gather_near(x, 0).start()
    for which in range(3):
        for i in range(nh):
            weights[i][which].start()
    rows[0, pl.ds(pl.multiple_of(c * t, t), t), :] = masked[...]
    rows[1, pl.ds(pl.multiple_of(c * t, t), t), :] = cot[...]

    def finish_gather(x):
        for j in range(1, Z):
            gather_far(x, j).wait_recv()
            gather_near(x, j).start()
        for j in range(Z):
            gather_near(x, j).wait_recv()

    def quarter(index):
        return pl.ds(pl.multiple_of(index * tq, tq), tq)

    def gu_copy(i, j):
        p = lax.rem(r + j, R)
        return remote(
            gu_send.at[i, :, quarter(p), :],
            gu_recv.at[i, j - 1],
            gu_ss.at[i, j],
            gu_rs.at[i, j],
            (p, c),
        )

    def gh_copy(i, j):
        p = lax.rem(r + j, R)
        return remote(
            gh_send.at[i, quarter(p), :],
            gh_recv.at[i, j - 1],
            gh_ss.at[i, j],
            gh_rs.at[i, j],
            (p, c),
        )

    def act_copy(a, i, j):
        p = lax.rem(r + j, R)
        return remote(
            act.at[a, i, quarter(r), :],
            act.at[a, i, quarter(r), :],
            act_ss.at[a, i, j],
            act_rs.at[a, i, j],
            (p, c),
        )

    finish_gather(0)
    for i in range(nh):
        weights[i][0].wait()
        weights[i][1].wait()

    def gate_up_step(i, carry):
        gu_send[i, 0] = dot(rows[0], gw[i]).astype(BF16)
        gu_send[i, 1] = dot(rows[0], uw[i]).astype(BF16)
        for j in range(1, R):
            gu_copy(i, j).start()
        return carry

    lax.fori_loop(0, nh, gate_up_step, 0)
    tok_out = pltpu.make_async_copy(rows.at[0], tok_hbm, o_sem.at[0])
    tok_out.start()

    finish_gather(1)
    for i in range(nh):
        weights[i][2].wait()

    def grad_hidden_step(i, carry):
        gh_send[i] = dot_last(rows[1], dw[i]).astype(BF16)
        for j in range(1, R):
            gh_copy(i, j).start()
        return carry

    lax.fori_loop(0, nh, grad_hidden_step, 0)
    cot_out = pltpu.make_async_copy(rows.at[1], cotall_hbm, o_sem.at[1])
    cot_out.start()

    def hidden_step(i, carry):
        for j in range(1, R):
            gu_copy(i, j).wait_recv()
        gate = gu_send[i, 0, quarter(r), :].astype(F32)
        up = gu_send[i, 1, quarter(r), :].astype(F32)
        for j in range(1, R):
            gate = gate + gu_recv[i, j - 1, 0].astype(F32)
            up = up + gu_recv[i, j - 1, 1].astype(F32)
        gate_s[i] = gate
        up_s[i] = up
        act[0, i, quarter(r), :] = (gate * jax.nn.sigmoid(gate) * up).astype(BF16)
        for j in range(1, R):
            act_copy(0, i, j).start()
        return carry

    lax.fori_loop(0, nh, hidden_step, 0)

    def dgate_step(i, carry):
        for j in range(1, R):
            gh_copy(i, j).wait_recv()
        grad = gh_send[i, quarter(r), :].astype(F32)
        for j in range(1, R):
            grad = grad + gh_recv[i, j - 1].astype(F32)
        gate = gate_s[i]
        sig = jax.nn.sigmoid(gate)
        act[1, i, quarter(r), :] = (
            grad * up_s[i] * sig * (1.0 + gate * (1.0 - sig))
        ).astype(BF16)
        act[2, i, quarter(r), :] = (grad * gate * sig).astype(BF16)
        for j in range(1, R):
            act_copy(1, i, j).start()
            act_copy(2, i, j).start()
        return carry

    lax.fori_loop(0, nh, dgate_step, 0)

    def near_sum(x, n):
        return remote(
            part.at[x, n, :, 1 - k],
            sib_recv.at[x, n],
            sib_ss.at[x, n],
            sib_rs.at[x, n],
            (r, sib),
        )

    def far_sum(x, n, j):
        zp = lax.rem(z + j, Z)
        return remote(
            z_send.at[x, n, zp],
            z_recv.at[x, n, j - 1],
            z_ss.at[x, n, j],
            z_rs.at[x, n, j],
            (r, zp * 2 + k),
        )

    def send_part(x, n, value):
        part[x, n] = value.astype(BF16).reshape(Z, 2, t, dchunk)
        near_sum(x, n).start()

    def pass_on(x, n):
        near_sum(x, n).wait_recv()
        z_send[x, n] = (part[x, n, :, k].astype(F32) + sib_recv[x, n].astype(F32)).astype(BF16)
        for j in range(1, Z):
            far_sum(x, n, j).start()

    def collect(x, n):
        for j in range(1, Z):
            far_sum(x, n, j).wait_recv()
        value = z_send[x, n, z].astype(F32)
        for j in range(1, Z):
            value = value + z_recv[x, n, j - 1].astype(F32)
        return value.astype(BF16)

    def act_wait(a):
        def step(i, carry):
            for j in range(1, R):
                act_copy(a, i, j).wait_recv()
            return carry

        lax.fori_loop(0, nh, step, 0)

    act_wait(0)
    hid_out = pltpu.make_async_copy(act.at[0], hid_hbm, o_sem.at[2])
    hid_out.start()
    for n in range(nd):
        cols = slice(n * dchunk, (n + 1) * dchunk)

        def out_step(i, total_value):
            return total_value + dot(act[0, i], dw[i, :, cols])

        send_part(0, n, lax.fori_loop(0, nh, out_step, jnp.zeros((total, dchunk), F32)))
        if n:
            pass_on(0, n - 1)
    pass_on(0, nd - 1)

    act_wait(1)
    dg_out = pltpu.make_async_copy(act.at[1], dg_hbm, o_sem.at[3])
    dg_out.start()
    act_wait(2)
    du_out = pltpu.make_async_copy(act.at[2], du_hbm, o_sem.at[4])
    du_out.start()
    for n in range(nd):
        cols = slice(n * dchunk, (n + 1) * dchunk)

        def mask_step(i, total_value):
            return (
                total_value
                + dot_last(act[1, i], gw[i, cols, :])
                + dot_last(act[2, i], uw[i, cols, :])
            )

        send_part(1, n, lax.fori_loop(0, nh, mask_step, jnp.zeros((total, dchunk), F32)))
        if n:
            pass_on(1, n - 1)
    pass_on(1, nd - 1)

    for n in range(nd):
        out[:, n * dchunk : (n + 1) * dchunk] = collect(0, n)
    for n in range(nd):
        gmask[:, n * dchunk : (n + 1) * dchunk] = collect(1, n)

    for x in range(2):
        for j in range(1, Z):
            gather_far(x, j).wait_send()
        for j in range(Z):
            gather_near(x, j).wait_send()
        for n in range(nd):
            near_sum(x, n).wait_send()
            for j in range(1, Z):
                far_sum(x, n, j).wait_send()

    def drain(i, carry):
        for j in range(1, R):
            gu_copy(i, j).wait_send()
            gh_copy(i, j).wait_send()
            for a in range(3):
                act_copy(a, i, j).wait_send()
        return carry

    lax.fori_loop(0, nh, drain, 0)
    for copy in (tok_out, cot_out, hid_out, dg_out, du_out):
        copy.wait()


def exchange(R, C, masked, cot, gate_weight, up_weight, down_weight):
    t, width = masked.shape
    hidden = gate_weight.shape[1]
    total = t * C
    tq = total // R
    Z = C // 2
    chunk = 256 if hidden % 256 == 0 else hidden
    dchunk = 512 if width % 512 == 0 else width
    nh, nd = hidden // chunk, width // dchunk
    dma = pltpu.SemaphoreType.DMA
    vmem = pl.BlockSpec(memory_space=pltpu.VMEM)
    anywhere = pl.BlockSpec(memory_space=pl.ANY)
    small = jax.ShapeDtypeStruct((t, width), BF16)
    wide = jax.ShapeDtypeStruct((total, width), BF16)
    units = jax.ShapeDtypeStruct((nh, total, chunk), BF16)
    return pl.pallas_call(
        functools.partial(exchange_kernel, R, C),
        out_shape=(small, small, wide, wide, units, units, units),
        in_specs=[vmem, vmem, anywhere, anywhere, anywhere],
        out_specs=(vmem, vmem) + (anywhere,) * 5,
        scratch_shapes=[
            pltpu.VMEM((nh, width, chunk), BF16),
            pltpu.VMEM((nh, width, chunk), BF16),
            pltpu.VMEM((nh, chunk, width), BF16),
            pltpu.VMEM((2, total, width), BF16),
            pltpu.VMEM((nh, 2, total, chunk), BF16),
            pltpu.VMEM((nh, R - 1, 2, tq, chunk), BF16),
            pltpu.VMEM((nh, total, chunk), BF16),
            pltpu.VMEM((nh, R - 1, tq, chunk), BF16),
            pltpu.VMEM((nh, tq, chunk), F32),
            pltpu.VMEM((nh, tq, chunk), F32),
            pltpu.VMEM((3, nh, total, chunk), BF16),
            pltpu.VMEM((2, nd, Z, 2, t, dchunk), BF16),
            pltpu.VMEM((2, nd, Z, t, dchunk), BF16),
            pltpu.VMEM((2, nd, Z, t, dchunk), BF16),
            pltpu.VMEM((2, nd, Z - 1, t, dchunk), BF16),
            dma((3, nh)),
            dma((5,)),
            dma((2, Z)),
            dma((2, Z)),
            dma((2, Z)),
            dma((2, Z)),
            dma((nh, R)),
            dma((nh, R)),
            dma((nh, R)),
            dma((nh, R)),
            dma((3, nh, R)),
            dma((3, nh, R)),
            dma((2, nd)),
            dma((2, nd)),
            dma((2, nd, Z)),
            dma((2, nd, Z)),
        ],
        compiler_params=pltpu.CompilerParams(
            collective_id=0, has_side_effects=True, vmem_limit_bytes=56 * 1024 * 1024
        ),
        cost_estimate=pl.CostEstimate(
            flops=12 * total * width * hidden, bytes_accessed=6 * width * hidden, transcendentals=0
        ),
    )(masked, cot, gate_weight, up_weight, down_weight)


def weight_grad_kernel(tok, cot, hid, dg, du, grad_gate, grad_up, grad_down, tok_t):
    @pl.when(pl.program_id(0) == 0)
    def _():
        tok_t[...] = tok[...].T

    grad_gate[...] = dot(tok_t[...], dg[0]).astype(BF16)
    grad_up[...] = dot(tok_t[...], du[0]).astype(BF16)
    grad_down[...] = lax.dot_general(
        hid[0], cot[...], FIRST, preferred_element_type=F32
    ).astype(BF16)


def weight_grads(tok, cot, hid, dg, du):
    total, width = tok.shape
    nh, _, chunk = hid.shape
    hidden = nh * chunk
    whole = pl.BlockSpec((total, width), lambda i: (0, 0))
    unit = pl.BlockSpec((1, total, chunk), lambda i: (i, 0, 0))
    across = jax.ShapeDtypeStruct((width, hidden), BF16)
    return pl.pallas_call(
        weight_grad_kernel,
        grid=(nh,),
        out_shape=(across, across, jax.ShapeDtypeStruct((hidden, width), BF16)),
        in_specs=[whole, whole, unit, unit, unit],
        out_specs=(
            pl.BlockSpec((width, chunk), lambda i: (0, i)),
            pl.BlockSpec((width, chunk), lambda i: (0, i)),
            pl.BlockSpec((chunk, width), lambda i: (i, 0)),
        ),
        scratch_shapes=[pltpu.VMEM((width, total), BF16)],
        compiler_params=pltpu.CompilerParams(vmem_limit_bytes=48 * 1024 * 1024),
        cost_estimate=pl.CostEstimate(
            flops=6 * total * width * hidden, bytes_accessed=6 * width * hidden, transcendentals=0
        ),
    )(tok, cot, hid, dg, du)


def shards(
    R,
    C,
    frames,
    cotangent,
    gate_weight,
    up_weight,
    down_weight,
    utt_ids,
    valid_len,
    time_start,
    time_width,
    freq_start,
    freq_width,
):
    tok_rows, feat_cols = frames.shape
    first_tok = lax.axis_index("col") * tok_rows
    first_feat = lax.axis_index("row") * feat_cols
    tok_index = first_tok + jnp.arange(tok_rows, dtype=jnp.int32)
    feat_index = first_feat + jnp.arange(feat_cols, dtype=jnp.int32)
    local_ids = lax.dynamic_slice_in_dim(utt_ids, first_tok, tok_rows)
    keep_mask, valid_rows = span_masks(
        utt_ids,
        local_ids,
        tok_index,
        feat_index,
        valid_len,
        time_start,
        time_width,
        freq_start,
        freq_width,
    )
    masked = jnp.where(keep_mask, frames, jnp.zeros_like(frames))
    cot_valid = jnp.where(valid_rows[:, None], cotangent, jnp.zeros_like(cotangent))
    output, grad_masked, tok, cot, hid, dg, du = exchange(
        R, C, masked, cot_valid, gate_weight, up_weight, down_weight
    )
    grad_gate, grad_up, grad_down = weight_grads(tok, cot, hid, dg, du)
    grad_frames = jnp.where(keep_mask, grad_masked, jnp.zeros_like(grad_masked))
    return (output, grad_frames, grad_gate, grad_up, grad_down)


def solution(mesh):
    placed = (
        P("col", "row"),
        P("col", "row"),
        P("row", "col"),
        P("row", "col"),
        P("col", "row"),
        P(),
        P(),
        P(),
        P(),
        P(),
        P(),
    )
    return jax.shard_map(
        functools.partial(shards, mesh.shape["row"], mesh.shape["col"]),
        mesh=mesh,
        in_specs=placed,
        out_specs=(
            P("col", "row"),
            P("col", "row"),
            P("row", "col"),
            P("row", "col"),
            P("col", "row"),
        ),
        check_vma=False,
    )
```

time: 234 us -> 132 us (0.56)
  waiting for transfers between devices: 123 us -> 0 us
  Pallas kernels: 0 us -> 119 us
  matrix products: 48.7 us -> 0 us
  blocking collectives: 36.5 us -> 0 us
  between operations: 14.2 us -> 0.68 us
  local copies, waits for them, and re-layouts: 0.78 us -> 7.4 us
  other arithmetic: 10.3 us -> 5.17 us
    pallas_call x0 -> x2, Pallas kernels: none -> 119 us  [the longest x1 109 us: exchange(): pl.pallas_call(functools.partial(exchange_kernel, R, C), out_shape=(small...]
    reduce_scatter x4 -> x0, waiting for transfers between devices: 87.8 us -> none  [the longest x1 29.8 us: shards(): lax.psum_scatter(jnp.concatenate([jnp.dot(block, gate_weight, preferred_e...]
    dot_general x9 -> x0, matrix products: 48.7 us -> none  [the longest x1 6.47 us: shards(): lax.dot_general(hidden_all, cot_all, contract_first, preferred_element_ty...]
    all_gather x3 -> x0, blocking collectives: 36.5 us -> none  [the longest x1 12.6 us: shards(): lax.all_gather(dup, 'row', axis=0, tiled=True)]
    all_gather x2 -> x0, waiting for transfers between devices: 35 us -> none  [the longest x1 23.2 us: shards(): tokens_all = lax.all_gather(masked, 'col', axis=0, tiled=True)]
    unnamed x10 -> x13, local copies, waits for them, and re-layouts: 0.02 us -> 6.64 us
    convert_element_type x3 -> x0, other arithmetic: 3.98 us -> none  [the longest x1 1.71 us: shards(): jnp.where(keep_mask, grad_masked, jnp.zeros_like(grad_masked))]
  transfers between devices with their start and end apart: 6 -> 0, of which waited for: 5 -> 0; matrix products, arithmetic and copies ran while one was open for 20% -> 0% of each run, Pallas kernels for 0% -> 0%
where the time goes in v1:
time: 132 us
  Pallas kernels  119 us (90%)
  local copies, waits for them, and re-layouts  7.4 us (6%)
  other arithmetic  5.17 us (4%)
    pallas_call x1, Pallas kernels, exchange(): pl.pallas_call(functools.partial(exchange_kernel, R, C), out_shape=(small...  109 us
    pallas_call x1, Pallas kernels, weight_grads(): pl.pallas_call(weight_grad_kernel, grid=(nh,), out_shape=(across, across,...  9.61 us
    unnamed x13, local copies, waits for them, and re-layouts  6.64 us

profile of v1, /device:TPU:0, one launch (start us, length us, event | category | flops | bytes accessed | tf_op | source)
XLA Modules:
  0.0 131.8 jit_solution(7595467043450955114)
XLA Ops:
  0.6 0.8 dynamic_slice.3
  1.4 0.8 convert_reduce_fusion
  2.2 0.8 select_reduce_fusion.4
  3.1 1.8 %broadcast_select_fusion = (bf16[32,2048]{1,0:T(8,128)(2,1)}, bf16[32,2048]{1,0:T(8,128)(2,1)}) fusion(bf16[32,2048]{1,0:T(8,128)(2,1)} %param.12, pred[32]{0:T(512)(128)(4,1)S(1)} %get-tuple-element.31, bf16[32,2048]{1,0:T(8,128)(2,1)} %param.11, s32[32]{0:T(128)S(1)} %add.47, s32[32]{0:T(128)S(1)} %get-tuple-element.27, s32[2048]{0:T(1024)S(1)} %iota_add_fusion, ...), kind=kLoop, calls=%fused_computation.1 | loop fusion | flops 458752 | bytes 532800 | tf_op jit(solution)/shard_map/jit(_where)/select_n | solution.py:520
  4.9 108.9 %shard_map.146 = (bf16[32,2048]{1,0:T(8,128)(2,1)}, bf16[32,2048]{1,0:T(8,128)(2,1)}, bf16[256,2048]{1,0:T(8,128)(2,1)}, bf16[256,2048]{1,0:T(8,128)(2,1)}, bf16...) custom-call(bf16[32,2048]{1,0:T(8,128)(2,1)} %get-tuple-element.34.masked, ...), custom_call_target="tpu_custom_call" | custom-call | flops 11274289152 | bytes 22020096 | tf_op jit(solution)/shard_map/pallas_call | solution.py:403
  113.8 1.7 %broadcast_select_fusion.1 = bf16[32,2048]{1,0:T(8,128)(2,1)} fusion(bf16[32,2048]{1,0:T(8,128)(2,1)} %get-tuple-element.16, s32[32]{0:T(128)S(1)} %add.47, s32[32]{0:T(128)S(1)} %get-tuple-element.27, s32[2048]{0:T(1024)S(1)} %iota_add_fusion, pred[32]{0:T(512)(128)(4,1)S(1)} %get-tuple-element.32), kind=kLoop, calls=%fused_computation.2 | loop fusion | flops 393216 | bytes 270624 | tf_op jit(solution)/shard_map/jit(_where)/select_n | solution.py:525
  115.5 0.0 copy-start
  115.5 1.2 copy-done
  116.7 0.0 copy-start.1
  116.7 1.2 copy-done.1
  118.0 0.0 copy-start.2
  118.0 1.2 copy-done.2
  119.2 0.0 copy-start.3
  119.2 1.2 copy-done.3
  120.3 0.0 copy-start.4
  120.3 1.2 copy-done.4
  121.5 0.0 copy-start.5
  121.5 9.6 %shard_map.147 = (bf16[2048,1792]{1,0:T(8,128)(2,1)}, bf16[2048,1792]{1,0:T(8,128)(2,1)}, bf16[1792,2048]{1,0:T(8,128)(2,1)}) custom-call(bf16[256,2048]{1,0:T(8,128)(2,1)S(1)} %copy-done, bf16[256,2048]{1,0:T(8,128)(2,1)S(1)} %copy-done.1, bf16[7,256,256]{2,1,0:T(8,128)(2,1)S(1)} %copy-done.2, bf16[7,256,256]{2,1,0:T(8,128)(2,1)S(1)} %copy-done.3, ...), custom_call_target="tpu_custom_call" | custom-call | flops 5637144576 | bytes 22020096 | tf_op jit(solution)/shard_map/pallas_call | solution.py:469
  131.1 0.0 copy-done.5
  131.1 0.7 copy.17
  (3 shorter events, 0.0 us)
Async XLA Ops:
  115.5 1.2 copy-start
  116.7 1.2 copy-start.1
  118.0 1.2 copy-start.2
  119.2 1.2 copy-start.3
  120.3 1.2 copy-start.4
  121.5 9.6 %copy-start.5 = (bf16[32,2048]{1,0:T(8,128)(2,1)S(1)}, bf16[32,2048]{1,0:T(8,128)(2,1)}, u32[]{:S(2)}) copy-start(bf16[32,2048]{1,0:T(8,128)(2,1)} %get-tuple-element.40) | copy-start | bytes 393220

commit v2 on v1

--- a/solution.py
+++ b/solution.py
@@ -72,8 +72,10 @@
     rows,
     gu_send,
     gu_recv,
+    gu_fwd,
     gh_send,
     gh_recv,
+    gh_fwd,
     gate_s,
     up_s,
     act,
@@ -161,10 +163,12 @@
         src = (masked, cot)[x] if j == 0 else block(x, index)
         return remote(src, block(x, index), fw_s.at[x, j], fw_r.at[x, j], (r, sib))
 
-    for x in range(2):
+    def start_gather(x):
         for j in range(1, Z):
             gather_far(x, j).start()
         gather_near(x, 0).start()
+
+    start_gather(0)
     for which in range(3):
         for i in range(nh):
             weights[i][which].start()
@@ -181,37 +185,97 @@
     def quarter(index):
         return pl.ds(pl.multiple_of(index * tq, tq), tq)
 
-    def gu_copy(i, j):
-        p = lax.rem(r + j, R)
+    square = R == 4
+    D = 2 if square else 1
+    h = tq // D
+    side = (r + 1 - 2 * (r % 2), r + 2 - 4 * (r // 2))
+    corner = 3 - r
+
+    def half(index, d):
+        return pl.ds(pl.multiple_of(index * tq + d * h, h), h)
+
+    def share(refs, i, index, d):
+        return refs[0].at[(i,) + (slice(None),) * (len(refs[0].shape) - 3) + (half(index, d),)]
+
+    def row_copy(refs, i, d, s):
+        send, recv, fwd, ss, rs = refs
+        if not square:
+            p = lax.rem(r + s + 1, R)
+            src = share(refs, i, p, 0)
+        elif s == 2:
+            p = side[1 - d]
+            src = fwd.at[i, d]
+        else:
+            p = side[d]
+            src = share(refs, i, (side[d], corner)[s], d)
+        return remote(src, recv.at[i, d, s], ss.at[i, d, s], rs.at[i, d, s], (p, c))
+
+    first_slots = (1, 0) if square else range(R - 1)
+    last_slots = (0, 2) if square else range(R - 1)
+
+    def row_start(refs, i):
+        for s in first_slots:
+            for d in range(D):
+                row_copy(refs, i, d, s).start()
+
+    def row_pass(refs, i):
+        if square:
+            for d in range(D):
+                row_copy(refs, i, d, 1).wait_recv()
+                mine = share(refs, i, side[1 - d], d)[...].astype(F32)
+                refs[2][i, d] = (mine + refs[1][i, d, 1].astype(F32)).astype(BF16)
+                row_copy(refs, i, d, 2).start()
+
+    def row_total(refs, i, d):
+        for s in last_slots:
+            row_copy(refs, i, d, s).wait_recv()
+        value = share(refs, i, r, d)[...].astype(F32)
+        for s in last_slots:
+            value = value + refs[1][i, d, s].astype(F32)
+        return value
+
+    gu = (gu_send, gu_recv, gu_fwd, gu_ss, gu_rs)
+    gh = (gh_send, gh_recv, gh_fwd, gh_ss, gh_rs)
+
+    def act_copy(a, i, s):
+        if not square:
+            p, rows_of = lax.rem(r + s + 1, R), quarter(r)
+        elif s < 2:
+            p, rows_of = side[s], quarter(r)
+        else:
+            p, rows_of = side[3 - s], half(side[s - 2], s - 2)
         return remote(
-            gu_send.at[i, :, quarter(p), :],
-            gu_recv.at[i, j - 1],
-            gu_ss.at[i, j],
-            gu_rs.at[i, j],
+            act.at[a, i, rows_of, :],
+            act.at[a, i, rows_of, :],
+            act_ss.at[a, i, s],
+            act_rs.at[a, i, s],
             (p, c),
         )
 
-    def gh_copy(i, j):
-        p = lax.rem(r + j, R)
-        return remote(
-            gh_send.at[i, quarter(p), :],
-            gh_recv.at[i, j - 1],
-            gh_ss.at[i, j],
-            gh_rs.at[i, j],
-            (p, c),
-        )
-
-    def act_copy(a, i, j):
-        p = lax.rem(r + j, R)
-        return remote(
-            act.at[a, i, quarter(r), :],
-            act.at[a, i, quarter(r), :],
-            act_ss.at[a, i, j],
-            act_rs.at[a, i, j],
-            (p, c),
-        )
+    act_slots = range(4) if square else range(R - 1)
+
+    def act_start(a, i):
+        for s in range(2) if square else act_slots:
+            act_copy(a, i, s).start()
+
+    def act_pass(a, i):
+        if square:
+            for s in range(2):
+                act_copy(a, i, s).wait_recv()
+                act_copy(a, i, s + 2).start()
+
+    def act_wait(a):
+        def step(i, carry):
+            for s in (2, 3) if square else act_slots:
+                act_copy(a, i, s).wait_recv()
+            return carry
+
+        lax.fori_loop(0, nh, step, 0)
+
+    lag = min(2, nh)
 
     finish_gather(0)
+    start_gather(1)
     for i in range(nh):
         weights[i][0].wait()
         weights[i][1].wait()
@@ -219,8 +283,12 @@
     def gate_up_step(i, carry):
         gu_send[i, 0] = dot(rows[0], gw[i]).astype(BF16)
         gu_send[i, 1] = dot(rows[0], uw[i]).astype(BF16)
-        for j in range(1, R):
-            gu_copy(i, j).start()
+        row_start(gu, i)
+
+        @pl.when(i >= lag)
+        def _():
+            row_pass(gu, i - lag)
+
         return carry
 
     lax.fori_loop(0, nh, gate_up_step, 0)
@@ -233,49 +301,56 @@
 
     def grad_hidden_step(i, carry):
         gh_send[i] = dot_last(rows[1], dw[i]).astype(BF16)
-        for j in range(1, R):
-            gh_copy(i, j).start()
+        row_start(gh, i)
+
+        @pl.when(i < lag)
+        def _():
+            row_pass(gu, nh - lag + i)
+
+        @pl.when(i >= lag)
+        def _():
+            row_pass(gh, i - lag)
+
+        for d in range(D):
+            both = row_total(gu, i, d)
+            gate, up = both[0], both[1]
+            gate_s[i, d] = gate
+            up_s[i, d] = up
+            act[0, i, half(r, d), :] = (gate * jax.nn.sigmoid(gate) * up).astype(BF16)
+        act_start(0, i)
         return carry
 
     lax.fori_loop(0, nh, grad_hidden_step, 0)
     cot_out = pltpu.make_async_copy(rows.at[1], cotall_hbm, o_sem.at[1])
     cot_out.start()
 
-    def hidden_step(i, carry):
-        for j in range(1, R):
-            gu_copy(i, j).wait_recv()
-        gate = gu_send[i, 0, quarter(r), :].astype(F32)
-        up = gu_send[i, 1, quarter(r), :].astype(F32)
-        for j in range(1, R):
-            gate = gate + gu_recv[i, j - 1, 0].astype(F32)
-            up = up + gu_recv[i, j - 1, 1].astype(F32)
-        gate_s[i] = gate
-        up_s[i] = up
-        act[0, i, quarter(r), :] = (gate * jax.nn.sigmoid(gate) * up).astype(BF16)
-        for j in range(1, R):
-            act_copy(0, i, j).start()
+    def dgate_step(i, carry):
+        @pl.when(i < lag)
+        def _():
+            row_pass(gh, nh - lag + i)
+
+        act_pass(0, i)
+        for d in range(D):
+            grad = row_total(gh, i, d)
+            gate = gate_s[i, d]
+            sig = jax.nn.sigmoid(gate)
+            act[1, i, half(r, d), :] = (
+                grad * up_s[i, d] * sig * (1.0 + gate * (1.0 - sig))
+            ).astype(BF16)
+            act[2, i, half(r, d), :] = (grad * gate * sig).astype(BF16)
+        act_start(1, i)
+        act_start(2, i)
         return carry
 
-    lax.fori_loop(0, nh, hidden_step, 0)
-
-    def dgate_step(i, carry):
-        for j in range(1, R):
-            gh_copy(i, j).wait_recv()
-        grad = gh_send[i, quarter(r), :].astype(F32)
-        for j in range(1, R):
-            grad = grad + gh_recv[i, j - 1].astype(F32)
-        gate = gate_s[i]
-        sig = jax.nn.sigmoid(gate)
-        act[1, i, quarter(r), :] = (
-            grad * up_s[i] * sig * (1.0 + gate * (1.0 - sig))
-        ).astype(BF16)
-        act[2, i, quarter(r), :] = (grad * gate * sig).astype(BF16)
-        for j in range(1, R):
-            act_copy(1, i, j).start()
-            act_copy(2, i, j).start()
-        return carry
-
     lax.fori_loop(0, nh, dgate_step, 0)
+
+    def grads_pass(low, high):
+        def step(i, carry):
+            act_pass(1, i)
+            act_pass(2, i)
+            return carry
+
+        lax.fori_loop(low, high, step, 0)
 
     def near_sum(x, n):
         return remote(
@@ -314,14 +389,6 @@
             value = value + z_recv[x, n, j - 1].astype(F32)
         return value.astype(BF16)
 
-    def act_wait(a):
-        def step(i, carry):
-            for j in range(1, R):
-                act_copy(a, i, j).wait_recv()
-            return carry
-
-        lax.fori_loop(0, nh, step, 0)
-
     act_wait(0)
     hid_out = pltpu.make_async_copy(act.at[0], hid_hbm, o_sem.at[2])
     hid_out.start()
@@ -332,6 +399,7 @@
             return total_value + dot(act[0, i], dw[i, :, cols])
 
         send_part(0, n, lax.fori_loop(0, nh, out_step, jnp.zeros((total, dchunk), F32)))
+        grads_pass(n * nh // nd, (n + 1) * nh // nd)
         if n:
             pass_on(0, n - 1)
     pass_on(0, nd - 1)
@@ -373,11 +441,13 @@
                 far_sum(x, n, j).wait_send()
 
     def drain(i, carry):
-        for j in range(1, R):
-            gu_copy(i, j).wait_send()
-            gh_copy(i, j).wait_send()
-            for a in range(3):
-                act_copy(a, i, j).wait_send()
+        for d in range(D):
+            for s in range(R - 1):
+                row_copy(gu, i, d, s).wait_send()
+                row_copy(gh, i, d, s).wait_send()
+        for a in range(3):
+            for s in act_slots:
+                act_copy(a, i, s).wait_send()
         return carry
 
     lax.fori_loop(0, nh, drain, 0)
@@ -390,6 +460,8 @@
     hidden = gate_weight.shape[1]
     total = t * C
     tq = total // R
+    D = 2 if R == 4 else 1
+    h = tq // D
     Z = C // 2
     chunk = 256 if hidden % 256 == 0 else hidden
     dchunk = 512 if width % 512 == 0 else width
@@ -411,11 +483,13 @@
             pltpu.VMEM((nh, chunk, width), BF16),
             pltpu.VMEM((2, total, width), BF16),
             pltpu.VMEM((nh, 2, total, chunk), BF16),
-            pltpu.VMEM((nh, R - 1, 2, tq, chunk), BF16),
+            pltpu.VMEM((nh, D, R - 1, 2, h, chunk), BF16),
+            pltpu.VMEM((nh, D, 2, h, chunk), BF16),
             pltpu.VMEM((nh, total, chunk), BF16),
-            pltpu.VMEM((nh, R - 1, tq, chunk), BF16),
-            pltpu.VMEM((nh, tq, chunk), F32),
-            pltpu.VMEM((nh, tq, chunk), F32),
+            pltpu.VMEM((nh, D, R - 1, h, chunk), BF16),
+            pltpu.VMEM((nh, D, h, chunk), BF16),
+            pltpu.VMEM((nh, D, h, chunk), F32),
+            pltpu.VMEM((nh, D, h, chunk), F32),
             pltpu.VMEM((3, nh, total, chunk), BF16),
             pltpu.VMEM((2, nd, Z, 2, t, dchunk), BF16),
             pltpu.VMEM((2, nd, Z, t, dchunk), BF16),
@@ -427,12 +501,12 @@
             dma((2, Z)),
             dma((2, Z)),
             dma((2, Z)),
-            dma((nh, R)),
-            dma((nh, R)),
-            dma((nh, R)),
-            dma((nh, R)),
-            dma((3, nh, R)),
-            dma((3, nh, R)),
+            dma((nh, D, R - 1)),
+            dma((nh, D, R - 1)),
+            dma((nh, D, R - 1)),
+            dma((nh, D, R - 1)),
+            dma((3, nh, max(R - 1, 4))),
+            dma((3, nh, max(R - 1, 4))),
             dma((2, nd)),
             dma((2, nd)),
             dma((2, nd, Z)),
@@ -477,7 +551,7 @@
             pl.BlockSpec((chunk, width), lambda i: (i, 0)),
         ),
         scratch_shapes=[pltpu.VMEM((width, total), BF16)],
-        compiler_params=pltpu.CompilerParams(vmem_limit_bytes=48 * 1024 * 1024),
+        compiler_params=pltpu.CompilerParams(vmem_limit_bytes=62 * 1024 * 1024),
         cost_estimate=pl.CostEstimate(
             flops=6 * total * width * hidden, bytes_accessed=6 * width * hidden, transcendentals=0
         ),

time: 132 us -> 115 us (0.87)
  Pallas kernels: 119 us -> 107 us
  local copies, waits for them, and re-layouts: 7.4 us -> 1.42 us
    pallas_call x1, Pallas kernels: 109 us -> 95 us  [exchange(): pl.pallas_call(functools.partial(exchange_kernel, R, C), out_shape=(small...]
    unnamed x13 -> x3, local copies, waits for them, and re-layouts: 6.64 us -> 0.66 us
    pallas_call x1, Pallas kernels: 9.61 us -> 12.1 us  [weight_grads(): pl.pallas_call(weight_grad_kernel, grid=(nh,), out_shape=(across, across,...]
where the time goes in v2:
time: 115 us; the launch traced here: 114 us
  Pallas kernels  107 us (93%)
  other arithmetic  5.17 us (4%)
  local copies, waits for them, and re-layouts  1.42 us (1%)
    pallas_call x1, Pallas kernels, exchange(): pl.pallas_call(functools.partial(exchange_kernel, R, C), out_shape=(small...  95 us
    pallas_call x1, Pallas kernels, weight_grads(): pl.pallas_call(weight_grad_kernel, grid=(nh,), out_shape=(across, across,...  12.1 us

profile of v2, /device:TPU:0, one launch (start us, length us, event | category | flops | bytes accessed | tf_op | source)
XLA Modules:
  0.0 114.4 jit_solution(2657332057849271777)
XLA Ops:
  0.6 0.8 dynamic_slice.3
  1.4 0.8 convert_reduce_fusion
  2.2 0.8 select_reduce_fusion.4
  3.1 1.8 %broadcast_select_fusion = (bf16[32,2048]{1,0:T(8,128)(2,1)}, bf16[32,2048]{1,0:T(8,128)(2,1)}) fusion(bf16[32,2048]{1,0:T(8,128)(2,1)} %param.12, pred[32]{0:T(512)(128)(4,1)S(1)} %get-tuple-element.31, bf16[32,2048]{1,0:T(8,128)(2,1)} %param.11, s32[32]{0:T(128)S(1)} %add.47, s32[32]{0:T(128)S(1)} %get-tuple-element.27, s32[2048]{0:T(1024)S(1)} %iota_add_fusion, ...), kind=kLoop, calls=%fused_computation.1 | loop fusion | flops 458752 | bytes 532800 | tf_op jit(solution)/shard_map/jit(_where)/select_n | solution.py:594
  4.9 95.0 %shard_map.146 = (bf16[32,2048]{1,0:T(8,128)(2,1)}, bf16[32,2048]{1,0:T(8,128)(2,1)}, bf16[256,2048]{1,0:T(8,128)(2,1)}, bf16[256,2048]{1,0:T(8,128)(2,1)}, bf16...) custom-call(bf16[32,2048]{1,0:T(8,128)(2,1)} %get-tuple-element.34.masked, ...), custom_call_target="tpu_custom_call" | custom-call | flops 11274289152 | bytes 22020096 | tf_op jit(solution)/shard_map/pallas_call | solution.py:475
  99.9 1.7 %broadcast_select_fusion.1 = bf16[32,2048]{1,0:T(8,128)(2,1)} fusion(bf16[32,2048]{1,0:T(8,128)(2,1)} %get-tuple-element.16, s32[32]{0:T(128)S(1)} %add.47, s32[32]{0:T(128)S(1)} %get-tuple-element.27, s32[2048]{0:T(1024)S(1)} %iota_add_fusion, pred[32]{0:T(512)(128)(4,1)S(1)} %get-tuple-element.32), kind=kLoop, calls=%fused_computation.2 | loop fusion | flops 393216 | bytes 270624 | tf_op jit(solution)/shard_map/jit(_where)/select_n | solution.py:599
  101.6 0.0 copy-start
  101.6 12.1 %shard_map.147 = (bf16[2048,1792]{1,0:T(8,128)(2,1)}, bf16[2048,1792]{1,0:T(8,128)(2,1)}, bf16[1792,2048]{1,0:T(8,128)(2,1)}) custom-call(bf16[256,2048]{1,0:T(8,128)(2,1)} %get-tuple-element.17.tok, bf16[256,2048]{1,0:T(8,128)(2,1)} %get-tuple-element.18.cot, bf16[7,256,256]{2,1,0:T(8,128)(2,1)} %get-tuple-element.19.hid, ...), custom_call_target="tpu_custom_call" | custom-call | flops 5637144576 | bytes 22020096 | tf_op jit(solution)/shard_map/pallas_call | solution.py:543
  113.7 0.0 copy-done
  113.7 0.7 copy.17
  (3 shorter events, 0.0 us)
Async XLA Ops:
  101.6 12.1 %copy-start = (bf16[32,2048]{1,0:T(8,128)(2,1)S(1)}, bf16[32,2048]{1,0:T(8,128)(2,1)}, u32[]{:S(2)}) copy-start(bf16[32,2048]{1,0:T(8,128)(2,1)} %get-tuple-element.40) | copy-start | bytes 393220
